TPU v7x, 512 devices: a whole 4x4x16 slice. The times are simulated.
512 devices in a mesh: ctx: 64 (over z, y), head: 8 (over x, core).
Axes of the slice: x: 4, y: 4, z: 16, core: 2. Of those that a mesh axis runs over, the one named last changes fastest.
Arguments:
- queries: bfloat16 [4096, 4096], P('ctx', 'head')
- cache_k: bfloat16 [32768, 1024], P('ctx', 'head')
- cache_v: bfloat16 [32768, 1024], P('ctx', 'head'), may hold values from -6 to 6
- new_k: bfloat16 [4096, 1024], P('ctx', 'head'), may hold values from -6 to 6
- new_v: bfloat16 [4096, 1024], P('ctx', 'head'), may hold values from -6 to 6
- counts: int32 [64], P('ctx'), may hold values from 1 to 64, as said below
- positions: int32 [4096], P('ctx'), may hold values from 0 to 4095, as said below
Outputs:
- attended: bfloat16 [4096, 4096], P(('ctx', 'head'))
Inputs may be any that keep to these rules, and one draw needn't show every extreme that they name: `counts`: every index of ctx has at least one live slot; some index has exactly 64. Live slots of ctx index c hold consecutive positions starting right after the last live position of index c - 1 (index 0 starts at 0); positions of other slots are arbitrary.
All inputs are finite; a program needn't handle non-finite values.
Results may differ from a plain program's by a relative error of at most 0.0055.
Values may be sent and summed in bfloat16 or wider, within the bound.
A program may use at most 128 MiB of HBM per device.

v0:
```python
import math

import jax
import jax.numpy as jnp
from jax import lax
from jax.sharding import PartitionSpec as P

HD = 128


def from_behind(value, axis, steps):
    count = lax.axis_size(axis)
    pairs = [(source, (source + steps) % count) for source in range(count)]
    return lax.ppermute(value, axis, pairs)


def absorb(best, denom, numer, scores, vals):
    best_new = jnp.maximum(best, jnp.max(scores, axis=-1))
    factor = jnp.exp(best - best_new)
    weights = jnp.exp(scores - best_new[..., None])
    denom = denom * factor + jnp.sum(weights, axis=-1)
    contrib = jnp.einsum(
        "rjgk,kjd->rjgd", weights.astype(jnp.bfloat16), vals, preferred_element_type=jnp.float32
    )
    numer = numer * factor[..., None] + contrib
    return (best_new, denom, numer)


def attend(
    qrows, qplace, best, denom, numer, keys_old, vals_old, keys_new, vals_new, key_place, key_live
):
    rows = qrows.shape[0]
    kvd = keys_old.shape[1]
    width = keys_old.shape[2]
    groups = qrows.shape[1] // (kvd * width)
    scale = 1.0 / math.sqrt(width)
    qfour = qrows.reshape(rows, kvd, groups, width)
    best = best.reshape(rows, kvd, groups)
    denom = denom.reshape(rows, kvd, groups)
    numer = numer.reshape(rows, kvd, groups, width)
    scores = (
        jnp.einsum("rjgd,kjd->rjgk", qfour, keys_old, preferred_element_type=jnp.float32) * scale
    )
    best, denom, numer = absorb(best, denom, numer, scores, vals_old)
    scores = (
        jnp.einsum("rjgd,kjd->rjgk", qfour, keys_new, preferred_element_type=jnp.float32) * scale
    )
    seen = key_live[None, :] & (key_place[None, :] <= qplace[:, None])
    scores = jnp.where(seen[:, None, None, :], scores, -jnp.inf)
    best, denom, numer = absorb(best, denom, numer, scores, vals_new)
    return (
        best.reshape(rows, kvd * groups),
        denom.reshape(rows, kvd * groups),
        numer.reshape(rows, -1),
    )


def local(queries, cache_k, cache_v, new_k, new_v, counts, positions):
    slots = queries.shape[0]
    columns = queries.shape[1]
    kvd = cache_k.shape[1] // HD
    groups = columns // (kvd * HD)
    keys_old = cache_k.reshape(-1, kvd, HD)
    vals_old = cache_v.reshape(-1, kvd, HD)
    keys_new = new_k.reshape(slots, kvd, HD)
    vals_new = new_v.reshape(slots, kvd, HD)
    key_place = positions.astype(jnp.float32)
    key_live = jnp.arange(slots, dtype=jnp.int32) < counts[0]
    stats = kvd * groups
    cycle_len = lax.axis_size("ctx")

    def turn(step, carry):
        qrows, qplace, numer, best, denom = carry
        best, denom, numer = attend(
            qrows,
            qplace,
            best,
            denom,
            numer,
            keys_old,
            vals_old,
            keys_new,
            vals_new,
            key_place,
            key_live,
        )
        qrows = from_behind(qrows, "ctx", 1)
        numer, best, denom, qplace = from_behind((numer, best, denom, qplace), "ctx", 1)
        return (qrows, qplace, numer, best, denom)

    start = (
        queries,
        key_place,
        jnp.zeros((slots, columns), jnp.float32),
        jnp.full((slots, stats), -jnp.inf, jnp.float32),
        jnp.zeros((slots, stats), jnp.float32),
    )
    final = lax.fori_loop(0, cycle_len, turn, start)
    numer_total = final[2].reshape(slots, stats, HD)
    denom_total = final[4]
    result = (numer_total / denom_total[..., None]).reshape(slots, columns)
    result = jnp.where(key_live[:, None], result, 0.0).astype(jnp.bfloat16)
    return lax.all_to_all(result, "head", split_axis=0, concat_axis=1, tiled=True)


def solution(mesh):
    return jax.shard_map(
        local,
        mesh=mesh,
        in_specs=(
            P("ctx", "head"),
            P("ctx", "head"),
            P("ctx", "head"),
            P("ctx", "head"),
            P("ctx", "head"),
            P("ctx"),
            P("ctx"),
        ),
        out_specs=P(("ctx", "head"), None),
        check_vma=False,
    )
```

profile of v0, /device:TPU:1, one launch (start us, length us, event | category | flops | bytes accessed | tf_op | source)
XLA Modules:
  0.0 1524.1 jit_solution(7620551565369332267)
XLA Ops:
  2.9 1368.1 %while.19 = (s32[]{:T(128)}, bf16[64,512]{1,0:T(8,128)(2,1)S(1)}, f32[64]{0:T(128)S(1)}, f32[64,512]{1,0:T(8,128)S(1)}, f32[64,4]{0,1:T(4,128)S(1)}, /*index=5*/...) while((s32[]{:T(128)}, bf16[64,512]{1,0:T(8,128)(2,1)S(1)}, ...), condition=%wide.region_5.6_spmd.clone, body=%wide.region_0.5_spmd.clone.sunk | while | flops 76538944 | bytes 4532709 | solution.py:98
  64.3 5.7 collective-permute-done.1
  79.5 5.7 collective-permute-start.4
  87.1 5.7 collective-permute-done.1
  102.4 5.7 collective-permute-start.4
  110.0 6.0 collective-permute-done.1
  132.0 5.7 collective-permute-done.1
  146.1 5.9 collective-permute-start.4
  154.0 5.7 collective-permute-done.1
  168.9 5.7 collective-permute-start.4
  176.6 5.7 collective-permute-done.1
  191.2 5.7 collective-permute-start.4
  198.8 5.7 collective-permute-done.1
  219.3 5.7 collective-permute-done.1
  240.0 5.7 collective-permute-done.1
  261.0 5.7 collective-permute-done.1
  275.4 5.7 collective-permute-start.4
  283.1 5.7 collective-permute-done.1
  303.8 5.7 collective-permute-done.1
  324.5 6.0 collective-permute-done.1
  345.4 5.7 collective-permute-done.1
  397.2 5.7 collective-permute-start.4
  404.8 5.7 collective-permute-done.1
  419.7 5.7 collective-permute-start.4
  427.4 5.7 collective-permute-done.1
  442.6 5.7 collective-permute-start.4
  450.3 5.7 collective-permute-done.1
  471.9 5.7 collective-permute-done.1
  493.4 5.7 collective-permute-done.1
  508.8 5.7 collective-permute-start.4
  530.6 5.7 collective-permute-start.4
  538.2 5.7 collective-permute-done.1
  559.3 5.8 collective-permute-done.1
  601.1 5.7 collective-permute-done.1
  616.2 5.7 collective-permute-start.4
  665.1 5.7 collective-permute-done.1
  737.2 5.8 collective-permute-start.4
  744.9 5.7 collective-permute-done.1
  759.4 5.9 collective-permute-start.4
  767.2 5.7 collective-permute-done.1
  782.4 5.7 collective-permute-start.4
  811.6 6.0 collective-permute-done.1
  826.2 5.7 collective-permute-start.4
  848.8 6.0 collective-permute-start.4
  856.8 5.7 collective-permute-done.1
  898.9 5.7 collective-permute-done.1
  913.1 5.7 collective-permute-start.4
  941.2 5.7 collective-permute-done.1
  955.6 5.7 collective-permute-start.4
  984.1 6.0 collective-permute-done.1
  1005.1 6.0 collective-permute-done.1
  1025.9 5.7 collective-permute-done.1
  1077.1 5.7 collective-permute-start.4
  1099.7 5.7 collective-permute-start.4
  1122.8 5.7 collective-permute-start.4
  1166.2 5.7 collective-permute-start.4
  1188.9 5.7 collective-permute-start.4
  1210.7 5.7 collective-permute-start.4
  1239.0 5.9 collective-permute-done.1
  1260.9 6.0 collective-permute-done.1
  1296.0 5.7 collective-permute-start.4
  1303.6 5.7 collective-permute-done.1
  1345.4 5.7 collective-permute-done.1
  1371.4 152.1 %all_to_all.19 = bf16[8,8,512]{2,1,0:T(8,128)(2,1)S(1)} all-to-all(bf16[8,8,512]{2,1,0:T(8,128)(2,1)S(1)} %fusion.28), channel_id=1, replica_groups=mesh['ctx'=64,'head'=8] {'head'}, dimensions={0} | all-to-all | bytes 131072 | tf_op jit(solution)/shard_map/all_to_all | solution.py:103
  (1683 shorter events, 1006.6 us)
Async XLA Ops:
  5.6 23.0 %collective-permute-start.2 = (f32[64,512]{1,0:T(8,128)S(1)}, f32[64,512]{1,0:T(8,128)S(1)}, u32[]{:S(2)}, u32[]{:S(2)}) collective-permute-start(f32[64,512]{1,0:T(8,128)S(1)} %bitcast.126), channel_id=1, source_target_pairs={{0,8},{8,16},{16,24},{24,32},{32,40},{40,48},{48,56},{56,64},{64,7... | collective-permute-start | bytes 393224 | tf_op jit(solution)/shard_map/while/body/eval_jaxpr/ppermute | solution.py:14
  9.6 19.0 %collective-permute-start = (bf16[64,512]{1,0:T(8,128)(2,1)S(1)}, bf16[64,512]{1,0:T(8,128)(2,1)S(1)}, u32[]{:S(2)}, u32[]{:S(2)}) collective-permute-start(bf16[64,512]{1,0:T(8,128)(2,1)S(1)} %copy.59), channel_id=1, source_target_pairs={{0,8},{8,16},{16,24},{24,32},{32,40},{40,48},{48,56},{56,64},{64,7... | collective-permute-start | bytes 196616 | tf_op jit(solution)/shard_map/while/body/eval_jaxpr/ppermute | solution.py:14
  51.0 19.0 %collective-permute-start.2 = (f32[64,512]{1,0:T(8,128)S(1)}, f32[64,512]{1,0:T(8,128)S(1)}, u32[]{:S(2)}, u32[]{:S(2)}) collective-permute-start(f32[64,512]{1,0:T(8,128)S(1)} %bitcast.126), channel_id=1, source_target_pairs={{0,8},{8,16},{16,24},{24,32},{32,40},{40,48},{48,56},{56,64},{64,7... | collective-permute-start | bytes 393224 | tf_op jit(solution)/shard_map/while/body/eval_jaxpr/ppermute | solution.py:14
  72.6 20.2 %collective-permute-start.2 = (f32[64,512]{1,0:T(8,128)S(1)}, f32[64,512]{1,0:T(8,128)S(1)}, u32[]{:S(2)}, u32[]{:S(2)}) collective-permute-start(f32[64,512]{1,0:T(8,128)S(1)} %bitcast.126), channel_id=1, source_target_pairs={{0,8},{8,16},{16,24},{24,32},{32,40},{40,48},{48,56},{56,64},{64,7... | collective-permute-start | bytes 393224 | tf_op jit(solution)/shard_map/while/body/eval_jaxpr/ppermute | solution.py:14
  74.6 18.2 %collective-permute-start = (bf16[64,512]{1,0:T(8,128)(2,1)S(1)}, bf16[64,512]{1,0:T(8,128)(2,1)S(1)}, u32[]{:S(2)}, u32[]{:S(2)}) collective-permute-start(bf16[64,512]{1,0:T(8,128)(2,1)S(1)} %copy.59), channel_id=1, source_target_pairs={{0,8},{8,16},{16,24},{24,32},{32,40},{40,48},{48,56},{56,64},{64,7... | collective-permute-start | bytes 196616 | tf_op jit(solution)/shard_map/while/body/eval_jaxpr/ppermute | solution.py:14
  95.5 20.5 %collective-permute-start.2 = (f32[64,512]{1,0:T(8,128)S(1)}, f32[64,512]{1,0:T(8,128)S(1)}, u32[]{:S(2)}, u32[]{:S(2)}) collective-permute-start(f32[64,512]{1,0:T(8,128)S(1)} %bitcast.126), channel_id=1, source_target_pairs={{0,8},{8,16},{16,24},{24,32},{32,40},{40,48},{48,56},{56,64},{64,7... | collective-permute-start | bytes 393224 | tf_op jit(solution)/shard_map/while/body/eval_jaxpr/ppermute | solution.py:14
  97.4 18.5 %collective-permute-start = (bf16[64,512]{1,0:T(8,128)(2,1)S(1)}, bf16[64,512]{1,0:T(8,128)(2,1)S(1)}, u32[]{:S(2)}, u32[]{:S(2)}) collective-permute-start(bf16[64,512]{1,0:T(8,128)(2,1)S(1)} %copy.59), channel_id=1, source_target_pairs={{0,8},{8,16},{16,24},{24,32},{32,40},{40,48},{48,56},{56,64},{64,7... | collective-permute-start | bytes 196616 | tf_op jit(solution)/shard_map/while/body/eval_jaxpr/ppermute | solution.py:14
  118.7 19.0 %collective-permute-start.2 = (f32[64,512]{1,0:T(8,128)S(1)}, f32[64,512]{1,0:T(8,128)S(1)}, u32[]{:S(2)}, u32[]{:S(2)}) collective-permute-start(f32[64,512]{1,0:T(8,128)S(1)} %bitcast.126), channel_id=1, source_target_pairs={{0,8},{8,16},{16,24},{24,32},{32,40},{40,48},{48,56},{56,64},{64,7... | collective-permute-start | bytes 393224 | tf_op jit(solution)/shard_map/while/body/eval_jaxpr/ppermute | solution.py:14
  140.4 19.3 %collective-permute-start.2 = (f32[64,512]{1,0:T(8,128)S(1)}, f32[64,512]{1,0:T(8,128)S(1)}, u32[]{:S(2)}, u32[]{:S(2)}) collective-permute-start(f32[64,512]{1,0:T(8,128)S(1)} %bitcast.126), channel_id=1, source_target_pairs={{0,8},{8,16},{16,24},{24,32},{32,40},{40,48},{48,56},{56,64},{64,7... | collective-permute-start | bytes 393224 | tf_op jit(solution)/shard_map/while/body/eval_jaxpr/ppermute | solution.py:14
  162.3 19.9 %collective-permute-start.2 = (f32[64,512]{1,0:T(8,128)S(1)}, f32[64,512]{1,0:T(8,128)S(1)}, u32[]{:S(2)}, u32[]{:S(2)}) collective-permute-start(f32[64,512]{1,0:T(8,128)S(1)} %bitcast.126), channel_id=1, source_target_pairs={{0,8},{8,16},{16,24},{24,32},{32,40},{40,48},{48,56},{56,64},{64,7... | collective-permute-start | bytes 393224 | tf_op jit(solution)/shard_map/while/body/eval_jaxpr/ppermute | solution.py:14
  164.3 18.0 %collective-permute-start = (bf16[64,512]{1,0:T(8,128)(2,1)S(1)}, bf16[64,512]{1,0:T(8,128)(2,1)S(1)}, u32[]{:S(2)}, u32[]{:S(2)}) collective-permute-start(bf16[64,512]{1,0:T(8,128)(2,1)S(1)} %copy.59), channel_id=1, source_target_pairs={{0,8},{8,16},{16,24},{24,32},{32,40},{40,48},{48,56},{56,64},{64,7... | collective-permute-start | bytes 196616 | tf_op jit(solution)/shard_map/while/body/eval_jaxpr/ppermute | solution.py:14
  184.9 19.5 %collective-permute-start.2 = (f32[64,512]{1,0:T(8,128)S(1)}, f32[64,512]{1,0:T(8,128)S(1)}, u32[]{:S(2)}, u32[]{:S(2)}) collective-permute-start(f32[64,512]{1,0:T(8,128)S(1)} %bitcast.126), channel_id=1, source_target_pairs={{0,8},{8,16},{16,24},{24,32},{32,40},{40,48},{48,56},{56,64},{64,7... | collective-permute-start | bytes 393224 | tf_op jit(solution)/shard_map/while/body/eval_jaxpr/ppermute | solution.py:14
  227.6 18.1 %collective-permute-start.2 = (f32[64,512]{1,0:T(8,128)S(1)}, f32[64,512]{1,0:T(8,128)S(1)}, u32[]{:S(2)}, u32[]{:S(2)}) collective-permute-start(f32[64,512]{1,0:T(8,128)S(1)} %bitcast.126), channel_id=1, source_target_pairs={{0,8},{8,16},{16,24},{24,32},{32,40},{40,48},{48,56},{56,64},{64,7... | collective-permute-start | bytes 393224 | tf_op jit(solution)/shard_map/while/body/eval_jaxpr/ppermute | solution.py:14
  248.4 18.2 %collective-permute-start.2 = (f32[64,512]{1,0:T(8,128)S(1)}, f32[64,512]{1,0:T(8,128)S(1)}, u32[]{:S(2)}, u32[]{:S(2)}) collective-permute-start(f32[64,512]{1,0:T(8,128)S(1)} %bitcast.126), channel_id=1, source_target_pairs={{0,8},{8,16},{16,24},{24,32},{32,40},{40,48},{48,56},{56,64},{64,7... | collective-permute-start | bytes 393224 | tf_op jit(solution)/shard_map/while/body/eval_jaxpr/ppermute | solution.py:14
  269.3 19.4 %collective-permute-start.2 = (f32[64,512]{1,0:T(8,128)S(1)}, f32[64,512]{1,0:T(8,128)S(1)}, u32[]{:S(2)}, u32[]{:S(2)}) collective-permute-start(f32[64,512]{1,0:T(8,128)S(1)} %bitcast.126), channel_id=1, source_target_pairs={{0,8},{8,16},{16,24},{24,32},{32,40},{40,48},{48,56},{56,64},{64,7... | collective-permute-start | bytes 393224 | tf_op jit(solution)/shard_map/while/body/eval_jaxpr/ppermute | solution.py:14
  291.5 18.0 %collective-permute-start.2 = (f32[64,512]{1,0:T(8,128)S(1)}, f32[64,512]{1,0:T(8,128)S(1)}, u32[]{:S(2)}, u32[]{:S(2)}) collective-permute-start(f32[64,512]{1,0:T(8,128)S(1)} %bitcast.126), channel_id=1, source_target_pairs={{0,8},{8,16},{16,24},{24,32},{32,40},{40,48},{48,56},{56,64},{64,7... | collective-permute-start | bytes 393224 | tf_op jit(solution)/shard_map/while/body/eval_jaxpr/ppermute | solution.py:14
  312.2 18.4 %collective-permute-start.2 = (f32[64,512]{1,0:T(8,128)S(1)}, f32[64,512]{1,0:T(8,128)S(1)}, u32[]{:S(2)}, u32[]{:S(2)}) collective-permute-start(f32[64,512]{1,0:T(8,128)S(1)} %bitcast.126), channel_id=1, source_target_pairs={{0,8},{8,16},{16,24},{24,32},{32,40},{40,48},{48,56},{56,64},{64,7... | collective-permute-start | bytes 393224 | tf_op jit(solution)/shard_map/while/body/eval_jaxpr/ppermute | solution.py:14
  333.2 17.8 %collective-permute-start.2 = (f32[64,512]{1,0:T(8,128)S(1)}, f32[64,512]{1,0:T(8,128)S(1)}, u32[]{:S(2)}, u32[]{:S(2)}) collective-permute-start(f32[64,512]{1,0:T(8,128)S(1)} %bitcast.126), channel_id=1, source_target_pairs={{0,8},{8,16},{16,24},{24,32},{32,40},{40,48},{48,56},{56,64},{64,7... | collective-permute-start | bytes 393224 | tf_op jit(solution)/shard_map/while/body/eval_jaxpr/ppermute | solution.py:14
  390.7 19.8 %collective-permute-start.2 = (f32[64,512]{1,0:T(8,128)S(1)}, f32[64,512]{1,0:T(8,128)S(1)}, u32[]{:S(2)}, u32[]{:S(2)}) collective-permute-start(f32[64,512]{1,0:T(8,128)S(1)} %bitcast.126), channel_id=1, source_target_pairs={{0,8},{8,16},{16,24},{24,32},{32,40},{40,48},{48,56},{56,64},{64,7... | collective-permute-start | bytes 393224 | tf_op jit(solution)/shard_map/while/body/eval_jaxpr/ppermute | solution.py:14
  392.7 17.9 %collective-permute-start = (bf16[64,512]{1,0:T(8,128)(2,1)S(1)}, bf16[64,512]{1,0:T(8,128)(2,1)S(1)}, u32[]{:S(2)}, u32[]{:S(2)}) collective-permute-start(bf16[64,512]{1,0:T(8,128)(2,1)S(1)} %copy.59), channel_id=1, source_target_pairs={{0,8},{8,16},{16,24},{24,32},{32,40},{40,48},{48,56},{56,64},{64,7... | collective-permute-start | bytes 196616 | tf_op jit(solution)/shard_map/while/body/eval_jaxpr/ppermute | solution.py:14
  413.2 19.8 %collective-permute-start.2 = (f32[64,512]{1,0:T(8,128)S(1)}, f32[64,512]{1,0:T(8,128)S(1)}, u32[]{:S(2)}, u32[]{:S(2)}) collective-permute-start(f32[64,512]{1,0:T(8,128)S(1)} %bitcast.126), channel_id=1, source_target_pairs={{0,8},{8,16},{16,24},{24,32},{32,40},{40,48},{48,56},{56,64},{64,7... | collective-permute-start | bytes 393224 | tf_op jit(solution)/shard_map/while/body/eval_jaxpr/ppermute | solution.py:14
  415.1 17.9 %collective-permute-start = (bf16[64,512]{1,0:T(8,128)(2,1)S(1)}, bf16[64,512]{1,0:T(8,128)(2,1)S(1)}, u32[]{:S(2)}, u32[]{:S(2)}) collective-permute-start(bf16[64,512]{1,0:T(8,128)(2,1)S(1)} %copy.59), channel_id=1, source_target_pairs={{0,8},{8,16},{16,24},{24,32},{32,40},{40,48},{48,56},{56,64},{64,7... | collective-permute-start | bytes 196616 | tf_op jit(solution)/shard_map/while/body/eval_jaxpr/ppermute | solution.py:14
  435.7 20.2 %collective-permute-start.2 = (f32[64,512]{1,0:T(8,128)S(1)}, f32[64,512]{1,0:T(8,128)S(1)}, u32[]{:S(2)}, u32[]{:S(2)}) collective-permute-start(f32[64,512]{1,0:T(8,128)S(1)} %bitcast.126), channel_id=1, source_target_pairs={{0,8},{8,16},{16,24},{24,32},{32,40},{40,48},{48,56},{56,64},{64,7... | collective-permute-start | bytes 393224 | tf_op jit(solution)/shard_map/while/body/eval_jaxpr/ppermute | solution.py:14
  437.7 18.3 %collective-permute-start = (bf16[64,512]{1,0:T(8,128)(2,1)S(1)}, bf16[64,512]{1,0:T(8,128)(2,1)S(1)}, u32[]{:S(2)}, u32[]{:S(2)}) collective-permute-start(bf16[64,512]{1,0:T(8,128)(2,1)S(1)} %copy.59), channel_id=1, source_target_pairs={{0,8},{8,16},{16,24},{24,32},{32,40},{40,48},{48,56},{56,64},{64,7... | collective-permute-start | bytes 196616 | tf_op jit(solution)/shard_map/while/body/eval_jaxpr/ppermute | solution.py:14
  458.6 18.9 %collective-permute-start.2 = (f32[64,512]{1,0:T(8,128)S(1)}, f32[64,512]{1,0:T(8,128)S(1)}, u32[]{:S(2)}, u32[]{:S(2)}) collective-permute-start(f32[64,512]{1,0:T(8,128)S(1)} %bitcast.126), channel_id=1, source_target_pairs={{0,8},{8,16},{16,24},{24,32},{32,40},{40,48},{48,56},{56,64},{64,7... | collective-permute-start | bytes 393224 | tf_op jit(solution)/shard_map/while/body/eval_jaxpr/ppermute | solution.py:14
  480.3 18.9 %collective-permute-start.2 = (f32[64,512]{1,0:T(8,128)S(1)}, f32[64,512]{1,0:T(8,128)S(1)}, u32[]{:S(2)}, u32[]{:S(2)}) collective-permute-start(f32[64,512]{1,0:T(8,128)S(1)} %bitcast.126), channel_id=1, source_target_pairs={{0,8},{8,16},{16,24},{24,32},{32,40},{40,48},{48,56},{56,64},{64,7... | collective-permute-start | bytes 393224 | tf_op jit(solution)/shard_map/while/body/eval_jaxpr/ppermute | solution.py:14
  501.8 20.3 %collective-permute-start.2 = (f32[64,512]{1,0:T(8,128)S(1)}, f32[64,512]{1,0:T(8,128)S(1)}, u32[]{:S(2)}, u32[]{:S(2)}) collective-permute-start(f32[64,512]{1,0:T(8,128)S(1)} %bitcast.126), channel_id=1, source_target_pairs={{0,8},{8,16},{16,24},{24,32},{32,40},{40,48},{48,56},{56,64},{64,7... | collective-permute-start | bytes 393224 | tf_op jit(solution)/shard_map/while/body/eval_jaxpr/ppermute | solution.py:14
  503.7 18.3 %collective-permute-start = (bf16[64,512]{1,0:T(8,128)(2,1)S(1)}, bf16[64,512]{1,0:T(8,128)(2,1)S(1)}, u32[]{:S(2)}, u32[]{:S(2)}) collective-permute-start(bf16[64,512]{1,0:T(8,128)(2,1)S(1)} %copy.59), channel_id=1, source_target_pairs={{0,8},{8,16},{16,24},{24,32},{32,40},{40,48},{48,56},{56,64},{64,7... | collective-permute-start | bytes 196616 | tf_op jit(solution)/shard_map/while/body/eval_jaxpr/ppermute | solution.py:14
  524.8 19.1 %collective-permute-start.2 = (f32[64,512]{1,0:T(8,128)S(1)}, f32[64,512]{1,0:T(8,128)S(1)}, u32[]{:S(2)}, u32[]{:S(2)}) collective-permute-start(f32[64,512]{1,0:T(8,128)S(1)} %bitcast.126), channel_id=1, source_target_pairs={{0,8},{8,16},{16,24},{24,32},{32,40},{40,48},{48,56},{56,64},{64,7... | collective-permute-start | bytes 393224 | tf_op jit(solution)/shard_map/while/body/eval_jaxpr/ppermute | solution.py:14
  546.6 18.5 %collective-permute-start.2 = (f32[64,512]{1,0:T(8,128)S(1)}, f32[64,512]{1,0:T(8,128)S(1)}, u32[]{:S(2)}, u32[]{:S(2)}) collective-permute-start(f32[64,512]{1,0:T(8,128)S(1)} %bitcast.126), channel_id=1, source_target_pairs={{0,8},{8,16},{16,24},{24,32},{32,40},{40,48},{48,56},{56,64},{64,7... | collective-permute-start | bytes 393224 | tf_op jit(solution)/shard_map/while/body/eval_jaxpr/ppermute | solution.py:14
  567.8 18.6 %collective-permute-start.2 = (f32[64,512]{1,0:T(8,128)S(1)}, f32[64,512]{1,0:T(8,128)S(1)}, u32[]{:S(2)}, u32[]{:S(2)}) collective-permute-start(f32[64,512]{1,0:T(8,128)S(1)} %bitcast.126), channel_id=1, source_target_pairs={{0,8},{8,16},{16,24},{24,32},{32,40},{40,48},{48,56},{56,64},{64,7... | collective-permute-start | bytes 393224 | tf_op jit(solution)/shard_map/while/body/eval_jaxpr/ppermute | solution.py:14
  609.5 20.0 %collective-permute-start.2 = (f32[64,512]{1,0:T(8,128)S(1)}, f32[64,512]{1,0:T(8,128)S(1)}, u32[]{:S(2)}, u32[]{:S(2)}) collective-permute-start(f32[64,512]{1,0:T(8,128)S(1)} %bitcast.126), channel_id=1, source_target_pairs={{0,8},{8,16},{16,24},{24,32},{32,40},{40,48},{48,56},{56,64},{64,7... | collective-permute-start | bytes 393224 | tf_op jit(solution)/shard_map/while/body/eval_jaxpr/ppermute | solution.py:14
  611.4 18.0 %collective-permute-start = (bf16[64,512]{1,0:T(8,128)(2,1)S(1)}, bf16[64,512]{1,0:T(8,128)(2,1)S(1)}, u32[]{:S(2)}, u32[]{:S(2)}) collective-permute-start(bf16[64,512]{1,0:T(8,128)(2,1)S(1)} %copy.59), channel_id=1, source_target_pairs={{0,8},{8,16},{16,24},{24,32},{32,40},{40,48},{48,56},{56,64},{64,7... | collective-permute-start | bytes 196616 | tf_op jit(solution)/shard_map/while/body/eval_jaxpr/ppermute | solution.py:14
  652.3 18.4 %collective-permute-start.2 = (f32[64,512]{1,0:T(8,128)S(1)}, f32[64,512]{1,0:T(8,128)S(1)}, u32[]{:S(2)}, u32[]{:S(2)}) collective-permute-start(f32[64,512]{1,0:T(8,128)S(1)} %bitcast.126), channel_id=1, source_target_pairs={{0,8},{8,16},{16,24},{24,32},{32,40},{40,48},{48,56},{56,64},{64,7... | collective-permute-start | bytes 393224 | tf_op jit(solution)/shard_map/while/body/eval_jaxpr/ppermute | solution.py:14
  731.1 19.5 %collective-permute-start.2 = (f32[64,512]{1,0:T(8,128)S(1)}, f32[64,512]{1,0:T(8,128)S(1)}, u32[]{:S(2)}, u32[]{:S(2)}) collective-permute-start(f32[64,512]{1,0:T(8,128)S(1)} %bitcast.126), channel_id=1, source_target_pairs={{0,8},{8,16},{16,24},{24,32},{32,40},{40,48},{48,56},{56,64},{64,7... | collective-permute-start | bytes 393224 | tf_op jit(solution)/shard_map/while/body/eval_jaxpr/ppermute | solution.py:14
  753.3 19.6 %collective-permute-start.2 = (f32[64,512]{1,0:T(8,128)S(1)}, f32[64,512]{1,0:T(8,128)S(1)}, u32[]{:S(2)}, u32[]{:S(2)}) collective-permute-start(f32[64,512]{1,0:T(8,128)S(1)} %bitcast.126), channel_id=1, source_target_pairs={{0,8},{8,16},{16,24},{24,32},{32,40},{40,48},{48,56},{56,64},{64,7... | collective-permute-start | bytes 393224 | tf_op jit(solution)/shard_map/while/body/eval_jaxpr/ppermute | solution.py:14
  775.6 20.1 %collective-permute-start.2 = (f32[64,512]{1,0:T(8,128)S(1)}, f32[64,512]{1,0:T(8,128)S(1)}, u32[]{:S(2)}, u32[]{:S(2)}) collective-permute-start(f32[64,512]{1,0:T(8,128)S(1)} %bitcast.126), channel_id=1, source_target_pairs={{0,8},{8,16},{16,24},{24,32},{32,40},{40,48},{48,56},{56,64},{64,7... | collective-permute-start | bytes 393224 | tf_op jit(solution)/shard_map/while/body/eval_jaxpr/ppermute | solution.py:14
  777.5 18.2 %collective-permute-start = (bf16[64,512]{1,0:T(8,128)(2,1)S(1)}, bf16[64,512]{1,0:T(8,128)(2,1)S(1)}, u32[]{:S(2)}, u32[]{:S(2)}) collective-permute-start(bf16[64,512]{1,0:T(8,128)(2,1)S(1)} %copy.59), channel_id=1, source_target_pairs={{0,8},{8,16},{16,24},{24,32},{32,40},{40,48},{48,56},{56,64},{64,7... | collective-permute-start | bytes 196616 | tf_op jit(solution)/shard_map/while/body/eval_jaxpr/ppermute | solution.py:14
  798.4 19.2 %collective-permute-start.2 = (f32[64,512]{1,0:T(8,128)S(1)}, f32[64,512]{1,0:T(8,128)S(1)}, u32[]{:S(2)}, u32[]{:S(2)}) collective-permute-start(f32[64,512]{1,0:T(8,128)S(1)} %bitcast.126), channel_id=1, source_target_pairs={{0,8},{8,16},{16,24},{24,32},{32,40},{40,48},{48,56},{56,64},{64,7... | collective-permute-start | bytes 393224 | tf_op jit(solution)/shard_map/while/body/eval_jaxpr/ppermute | solution.py:14
  820.3 19.2 %collective-permute-start.2 = (f32[64,512]{1,0:T(8,128)S(1)}, f32[64,512]{1,0:T(8,128)S(1)}, u32[]{:S(2)}, u32[]{:S(2)}) collective-permute-start(f32[64,512]{1,0:T(8,128)S(1)} %bitcast.126), channel_id=1, source_target_pairs={{0,8},{8,16},{16,24},{24,32},{32,40},{40,48},{48,56},{56,64},{64,7... | collective-permute-start | bytes 393224 | tf_op jit(solution)/shard_map/while/body/eval_jaxpr/ppermute | solution.py:14
  842.2 20.2 %collective-permute-start.2 = (f32[64,512]{1,0:T(8,128)S(1)}, f32[64,512]{1,0:T(8,128)S(1)}, u32[]{:S(2)}, u32[]{:S(2)}) collective-permute-start(f32[64,512]{1,0:T(8,128)S(1)} %bitcast.126), channel_id=1, source_target_pairs={{0,8},{8,16},{16,24},{24,32},{32,40},{40,48},{48,56},{56,64},{64,7... | collective-permute-start | bytes 393224 | tf_op jit(solution)/shard_map/while/body/eval_jaxpr/ppermute | solution.py:14
  844.1 18.3 %collective-permute-start = (bf16[64,512]{1,0:T(8,128)(2,1)S(1)}, bf16[64,512]{1,0:T(8,128)(2,1)S(1)}, u32[]{:S(2)}, u32[]{:S(2)}) collective-permute-start(bf16[64,512]{1,0:T(8,128)(2,1)S(1)} %copy.59), channel_id=1, source_target_pairs={{0,8},{8,16},{16,24},{24,32},{32,40},{40,48},{48,56},{56,64},{64,7... | collective-permute-start | bytes 196616 | tf_op jit(solution)/shard_map/while/body/eval_jaxpr/ppermute | solution.py:14
  865.1 18.8 %collective-permute-start.2 = (f32[64,512]{1,0:T(8,128)S(1)}, f32[64,512]{1,0:T(8,128)S(1)}, u32[]{:S(2)}, u32[]{:S(2)}) collective-permute-start(f32[64,512]{1,0:T(8,128)S(1)} %bitcast.126), channel_id=1, source_target_pairs={{0,8},{8,16},{16,24},{24,32},{32,40},{40,48},{48,56},{56,64},{64,7... | collective-permute-start | bytes 393224 | tf_op jit(solution)/shard_map/while/body/eval_jaxpr/ppermute | solution.py:14
  886.7 17.9 %collective-permute-start.2 = (f32[64,512]{1,0:T(8,128)S(1)}, f32[64,512]{1,0:T(8,128)S(1)}, u32[]{:S(2)}, u32[]{:S(2)}) collective-permute-start(f32[64,512]{1,0:T(8,128)S(1)} %bitcast.126), channel_id=1, source_target_pairs={{0,8},{8,16},{16,24},{24,32},{32,40},{40,48},{48,56},{56,64},{64,7... | collective-permute-start | bytes 393224 | tf_op jit(solution)/shard_map/while/body/eval_jaxpr/ppermute | solution.py:14
  907.3 19.1 %collective-permute-start.2 = (f32[64,512]{1,0:T(8,128)S(1)}, f32[64,512]{1,0:T(8,128)S(1)}, u32[]{:S(2)}, u32[]{:S(2)}) collective-permute-start(f32[64,512]{1,0:T(8,128)S(1)} %bitcast.126), channel_id=1, source_target_pairs={{0,8},{8,16},{16,24},{24,32},{32,40},{40,48},{48,56},{56,64},{64,7... | collective-permute-start | bytes 393224 | tf_op jit(solution)/shard_map/while/body/eval_jaxpr/ppermute | solution.py:14
  929.1 17.8 %collective-permute-start.2 = (f32[64,512]{1,0:T(8,128)S(1)}, f32[64,512]{1,0:T(8,128)S(1)}, u32[]{:S(2)}, u32[]{:S(2)}) collective-permute-start(f32[64,512]{1,0:T(8,128)S(1)} %bitcast.126), channel_id=1, source_target_pairs={{0,8},{8,16},{16,24},{24,32},{32,40},{40,48},{48,56},{56,64},{64,7... | collective-permute-start | bytes 393224 | tf_op jit(solution)/shard_map/while/body/eval_jaxpr/ppermute | solution.py:14
  949.6 19.3 %collective-permute-start.2 = (f32[64,512]{1,0:T(8,128)S(1)}, f32[64,512]{1,0:T(8,128)S(1)}, u32[]{:S(2)}, u32[]{:S(2)}) collective-permute-start(f32[64,512]{1,0:T(8,128)S(1)} %bitcast.126), channel_id=1, source_target_pairs={{0,8},{8,16},{16,24},{24,32},{32,40},{40,48},{48,56},{56,64},{64,7... | collective-permute-start | bytes 393224 | tf_op jit(solution)/shard_map/while/body/eval_jaxpr/ppermute | solution.py:14
  971.7 18.4 %collective-permute-start.2 = (f32[64,512]{1,0:T(8,128)S(1)}, f32[64,512]{1,0:T(8,128)S(1)}, u32[]{:S(2)}, u32[]{:S(2)}) collective-permute-start(f32[64,512]{1,0:T(8,128)S(1)} %bitcast.126), channel_id=1, source_target_pairs={{0,8},{8,16},{16,24},{24,32},{32,40},{40,48},{48,56},{56,64},{64,7... | collective-permute-start | bytes 393224 | tf_op jit(solution)/shard_map/while/body/eval_jaxpr/ppermute | solution.py:14
  992.8 18.3 %collective-permute-start.2 = (f32[64,512]{1,0:T(8,128)S(1)}, f32[64,512]{1,0:T(8,128)S(1)}, u32[]{:S(2)}, u32[]{:S(2)}) collective-permute-start(f32[64,512]{1,0:T(8,128)S(1)} %bitcast.126), channel_id=1, source_target_pairs={{0,8},{8,16},{16,24},{24,32},{32,40},{40,48},{48,56},{56,64},{64,7... | collective-permute-start | bytes 393224 | tf_op jit(solution)/shard_map/while/body/eval_jaxpr/ppermute | solution.py:14
  1013.7 17.8 %collective-permute-start.2 = (f32[64,512]{1,0:T(8,128)S(1)}, f32[64,512]{1,0:T(8,128)S(1)}, u32[]{:S(2)}, u32[]{:S(2)}) collective-permute-start(f32[64,512]{1,0:T(8,128)S(1)} %bitcast.126), channel_id=1, source_target_pairs={{0,8},{8,16},{16,24},{24,32},{32,40},{40,48},{48,56},{56,64},{64,7... | collective-permute-start | bytes 393224 | tf_op jit(solution)/shard_map/while/body/eval_jaxpr/ppermute | solution.py:14
  1070.9 19.5 %collective-permute-start.2 = (f32[64,512]{1,0:T(8,128)S(1)}, f32[64,512]{1,0:T(8,128)S(1)}, u32[]{:S(2)}, u32[]{:S(2)}) collective-permute-start(f32[64,512]{1,0:T(8,128)S(1)} %bitcast.126), channel_id=1, source_target_pairs={{0,8},{8,16},{16,24},{24,32},{32,40},{40,48},{48,56},{56,64},{64,7... | collective-permute-start | bytes 393224 | tf_op jit(solution)/shard_map/while/body/eval_jaxpr/ppermute | solution.py:14
  1093.1 20.0 %collective-permute-start.2 = (f32[64,512]{1,0:T(8,128)S(1)}, f32[64,512]{1,0:T(8,128)S(1)}, u32[]{:S(2)}, u32[]{:S(2)}) collective-permute-start(f32[64,512]{1,0:T(8,128)S(1)} %bitcast.126), channel_id=1, source_target_pairs={{0,8},{8,16},{16,24},{24,32},{32,40},{40,48},{48,56},{56,64},{64,7... | collective-permute-start | bytes 393224 | tf_op jit(solution)/shard_map/while/body/eval_jaxpr/ppermute | solution.py:14
  1095.0 18.0 %collective-permute-start = (bf16[64,512]{1,0:T(8,128)(2,1)S(1)}, bf16[64,512]{1,0:T(8,128)(2,1)S(1)}, u32[]{:S(2)}, u32[]{:S(2)}) collective-permute-start(bf16[64,512]{1,0:T(8,128)(2,1)S(1)} %copy.59), channel_id=1, source_target_pairs={{0,8},{8,16},{16,24},{24,32},{32,40},{40,48},{48,56},{56,64},{64,7... | collective-permute-start | bytes 196616 | tf_op jit(solution)/shard_map/while/body/eval_jaxpr/ppermute | solution.py:14
  1115.7 20.4 %collective-permute-start.2 = (f32[64,512]{1,0:T(8,128)S(1)}, f32[64,512]{1,0:T(8,128)S(1)}, u32[]{:S(2)}, u32[]{:S(2)}) collective-permute-start(f32[64,512]{1,0:T(8,128)S(1)} %bitcast.126), channel_id=1, source_target_pairs={{0,8},{8,16},{16,24},{24,32},{32,40},{40,48},{48,56},{56,64},{64,7... | collective-permute-start | bytes 393224 | tf_op jit(solution)/shard_map/while/body/eval_jaxpr/ppermute | solution.py:14
  1117.6 18.5 %collective-permute-start = (bf16[64,512]{1,0:T(8,128)(2,1)S(1)}, bf16[64,512]{1,0:T(8,128)(2,1)S(1)}, u32[]{:S(2)}, u32[]{:S(2)}) collective-permute-start(bf16[64,512]{1,0:T(8,128)(2,1)S(1)} %copy.59), channel_id=1, source_target_pairs={{0,8},{8,16},{16,24},{24,32},{32,40},{40,48},{48,56},{56,64},{64,7... | collective-permute-start | bytes 196616 | tf_op jit(solution)/shard_map/while/body/eval_jaxpr/ppermute | solution.py:14
  1138.8 18.7 %collective-permute-start.2 = (f32[64,512]{1,0:T(8,128)S(1)}, f32[64,512]{1,0:T(8,128)S(1)}, u32[]{:S(2)}, u32[]{:S(2)}) collective-permute-start(f32[64,512]{1,0:T(8,128)S(1)} %bitcast.126), channel_id=1, source_target_pairs={{0,8},{8,16},{16,24},{24,32},{32,40},{40,48},{48,56},{56,64},{64,7... | collective-permute-start | bytes 393224 | tf_op jit(solution)/shard_map/while/body/eval_jaxpr/ppermute | solution.py:14
  1160.3 19.2 %collective-permute-start.2 = (f32[64,512]{1,0:T(8,128)S(1)}, f32[64,512]{1,0:T(8,128)S(1)}, u32[]{:S(2)}, u32[]{:S(2)}) collective-permute-start(f32[64,512]{1,0:T(8,128)S(1)} %bitcast.126), channel_id=1, source_target_pairs={{0,8},{8,16},{16,24},{24,32},{32,40},{40,48},{48,56},{56,64},{64,7... | collective-permute-start | bytes 393224 | tf_op jit(solution)/shard_map/while/body/eval_jaxpr/ppermute | solution.py:14
  1182.2 20.0 %collective-permute-start.2 = (f32[64,512]{1,0:T(8,128)S(1)}, f32[64,512]{1,0:T(8,128)S(1)}, u32[]{:S(2)}, u32[]{:S(2)}) collective-permute-start(f32[64,512]{1,0:T(8,128)S(1)} %bitcast.126), channel_id=1, source_target_pairs={{0,8},{8,16},{16,24},{24,32},{32,40},{40,48},{48,56},{56,64},{64,7... | collective-permute-start | bytes 393224 | tf_op jit(solution)/shard_map/while/body/eval_jaxpr/ppermute | solution.py:14
  1184.1 18.0 %collective-permute-start = (bf16[64,512]{1,0:T(8,128)(2,1)S(1)}, bf16[64,512]{1,0:T(8,128)(2,1)S(1)}, u32[]{:S(2)}, u32[]{:S(2)}) collective-permute-start(bf16[64,512]{1,0:T(8,128)(2,1)S(1)} %copy.59), channel_id=1, source_target_pairs={{0,8},{8,16},{16,24},{24,32},{32,40},{40,48},{48,56},{56,64},{64,7... | collective-permute-start | bytes 196616 | tf_op jit(solution)/shard_map/while/body/eval_jaxpr/ppermute | solution.py:14
  1204.9 19.2 %collective-permute-start.2 = (f32[64,512]{1,0:T(8,128)S(1)}, f32[64,512]{1,0:T(8,128)S(1)}, u32[]{:S(2)}, u32[]{:S(2)}) collective-permute-start(f32[64,512]{1,0:T(8,128)S(1)} %bitcast.126), channel_id=1, source_target_pairs={{0,8},{8,16},{16,24},{24,32},{32,40},{40,48},{48,56},{56,64},{64,7... | collective-permute-start | bytes 393224 | tf_op jit(solution)/shard_map/while/body/eval_jaxpr/ppermute | solution.py:14
  1226.8 18.1 %collective-permute-start.2 = (f32[64,512]{1,0:T(8,128)S(1)}, f32[64,512]{1,0:T(8,128)S(1)}, u32[]{:S(2)}, u32[]{:S(2)}) collective-permute-start(f32[64,512]{1,0:T(8,128)S(1)} %bitcast.126), channel_id=1, source_target_pairs={{0,8},{8,16},{16,24},{24,32},{32,40},{40,48},{48,56},{56,64},{64,7... | collective-permute-start | bytes 393224 | tf_op jit(solution)/shard_map/while/body/eval_jaxpr/ppermute | solution.py:14
  1247.6 19.3 %collective-permute-start.2 = (f32[64,512]{1,0:T(8,128)S(1)}, f32[64,512]{1,0:T(8,128)S(1)}, u32[]{:S(2)}, u32[]{:S(2)}) collective-permute-start(f32[64,512]{1,0:T(8,128)S(1)} %bitcast.126), channel_id=1, source_target_pairs={{0,8},{8,16},{16,24},{24,32},{32,40},{40,48},{48,56},{56,64},{64,7... | collective-permute-start | bytes 393224 | tf_op jit(solution)/shard_map/while/body/eval_jaxpr/ppermute | solution.py:14
  1289.6 19.7 %collective-permute-start.2 = (f32[64,512]{1,0:T(8,128)S(1)}, f32[64,512]{1,0:T(8,128)S(1)}, u32[]{:S(2)}, u32[]{:S(2)}) collective-permute-start(f32[64,512]{1,0:T(8,128)S(1)} %bitcast.126), channel_id=1, source_target_pairs={{0,8},{8,16},{16,24},{24,32},{32,40},{40,48},{48,56},{56,64},{64,7... | collective-permute-start | bytes 393224 | tf_op jit(solution)/shard_map/while/body/eval_jaxpr/ppermute | solution.py:14
  1332.3 18.7 %collective-permute-start.2 = (f32[64,512]{1,0:T(8,128)S(1)}, f32[64,512]{1,0:T(8,128)S(1)}, u32[]{:S(2)}, u32[]{:S(2)}) collective-permute-start(f32[64,512]{1,0:T(8,128)S(1)} %bitcast.126), channel_id=1, source_target_pairs={{0,8},{8,16},{16,24},{24,32},{32,40},{40,48},{48,56},{56,64},{64,7... | collective-permute-start | bytes 393224 | tf_op jit(solution)/shard_map/while/body/eval_jaxpr/ppermute | solution.py:14
  (323 other events, 2986.8 us)
where the time goes:
time: 1540 us; the launch traced here: 1520 us
  starting transfers between devices  825 us (54%)
  waiting for transfers between devices  366 us (24%)
  blocking collectives  152 us (10%)
  other arithmetic  66.2 us (4%)
  matrix products  64.4 us (4%)
  local copies, waits for them, and re-layouts  38.9 us (3%)
    ppermute x320, starting transfers between devices, from_behind(): return lax.ppermute(value, axis, pairs)  825 us
    ppermute x320, waiting for transfers between devices, from_behind(): return lax.ppermute(value, axis, pairs)  366 us
    all_to_all x1, blocking collectives, local(): lax.all_to_all(result, 'head', split_axis=0, concat_axis=1, tiled=True)  152 us
    lt x65, other arithmetic, local(): key_live = jnp.arange(slots, dtype=jnp.int32) < counts[0]  41.7 us
    dot_general x128, matrix products, absorb(): jnp.einsum('rjgk,kjd->rjgd', weights.astype(jnp.bfloat16), vals, preferre...  31.6 us
  transfers between devices with their start and end apart: 320, of which 73 were waited for; matrix products, arithmetic and copies ran while one was open for 0% of the time, Pallas kernels for 0%

commit v1 on v0

v1 whole, which is shorter than its diff:
```python
import functools
import math

import jax
import jax.numpy as jnp
from jax import lax
from jax.experimental import pallas as pl
from jax.experimental.pallas import tpu as pltpu
from jax.sharding import PartitionSpec as P

HD = 128
NY = 4
MESH = pl.DeviceIdType.MESH
F32 = jnp.float32
BF16 = jnp.bfloat16
LOW = -1e30
PIECES = 2


def kernel(
    nz, nh, q_ref, ck_ref, cv_ref, nk_ref, nv_ref, count_ref, pos_ref, out_ref,
    qall, kk, vbuf, nvbuf, vt, bias, scores, probs,
    st_num, st_stat, pin, min_, pout, mout, give, got,
    qsend, qrecv, ysend, yrecv, fsend, frecv, psend, precv, msend, mrecv, asend, arecv,
):
    slots = q_ref.shape[0]
    group = q_ref.shape[1] // HD
    rows = slots * group
    deep = ck_ref.shape[0]
    old = NY * deep
    near = nz // 4
    keys = old + NY * slots
    part = rows // PIECES
    depth = HD // PIECES
    tile = 2 * HD
    ctx = lax.axis_index("ctx")
    head = lax.axis_index("head")
    z = ctx // NY
    y = lax.rem(ctx, NY)

    def wrap(value):
        return lax.rem(value + 2 * nz, nz)

    def at_z(value):
        return (wrap(value) * NY + y, head)

    def at_y(value):
        return (z * NY + lax.rem(value + NY, NY), head)

    def remote(src, dst, send, recv, device):
        return pltpu.make_async_remote_copy(
            src_ref=src, dst_ref=dst, send_sem=send, recv_sem=recv, device_id=device, device_id_type=MESH
        )

    barrier = pltpu.get_barrier_semaphore()
    friends = [at_z(z + 1), at_z(z - 1), at_z(z + near + 1), at_z(z - near - 1), at_y(y + 1), at_y(y - 1)]
    friends += [(ctx, lax.rem(head + k, nh)) for k in range(1, nh)]
    for friend in friends:
        pl.semaphore_signal(barrier, inc=1, device_id=friend, device_id_type=MESH)

    count = count_ref[0]
    own = jnp.concatenate([q_ref[:, g * HD : (g + 1) * HD].astype(F32) for g in range(group)], axis=0)
    qall[z] = own.T.astype(BF16)
    live = lax.broadcasted_iota(jnp.int32, (slots, HD), 0) < count
    newk = nk_ref[...].astype(F32)
    kk[old : old + slots, :] = jnp.where(live, newk, jnp.broadcast_to(newk[0:1, :], newk.shape)).astype(BF16)
    nvbuf[0, :, 0:HD] = jnp.where(live, nv_ref[...].astype(F32), 0.0).astype(BF16)
    nvbuf[0, :, HD:] = jnp.where(live, 1.0, 0.0).astype(BF16)
    pl.semaphore_wait(barrier, len(friends))

    def kv_part(i, k):
        if i == 0:
            return kk.at[k * deep : (k + 1) * deep, :] if k else ck_ref
        if i == 1:
            return kk.at[old + k * slots : old + (k + 1) * slots, :]
        if i == 2:
            return vbuf.at[k] if k else cv_ref
        return nvbuf.at[k]

    def y_copy(way, i):
        device = at_y(y + 1) if way == 0 else at_y(y - 1)
        return remote(kv_part(i, 0), kv_part(i, 1 + way), ysend.at[way, i], yrecv.at[way, i], device)

    def f_copy(i):
        device = at_y(y + 1) if i < 2 else at_y(y - 1)
        return remote(kv_part(i, 1 if i < 2 else 2), kv_part(i, 3), fsend.at[i], frecv.at[i], device)

    def q_copy(way, lane, step, piece, owner, hop=1):
        device = at_z(z + hop) if way == 0 else at_z(z - hop)
        ref = qall.at[owner, pl.ds(piece * depth, depth), :]
        return remote(ref, ref, qsend.at[way, lane, step, piece], qrecv.at[way, lane, step, piece], device)

    for i in range(4):
        for way in (0, 1):
            if i == 0:
                for piece in range(PIECES):
                    q_copy(way, 0, 0, piece, z).start()
                for piece in range(PIECES):
                    q_copy(way, 1, 0, piece, z, near + 1).start()
            y_copy(way, i).start()

    def values_in(k, values_of):
        span = slice(k * deep, (k + 1) * deep)
        vt[0:HD, span] = values_of[...].astype(F32).T.astype(BF16)

    rate = math.log2(math.e) / math.sqrt(HD)

    def attend(one, two, kinds, first, last):
        wide = jnp.concatenate([qall[one], qall[two]], axis=1)
        before = jnp.concatenate([st_stat[one, 0:1, :], st_stat[two, 0:1, :]], axis=1)
        scores[first:last, :] = jnp.dot(kk[first:last, :], wide, preferred_element_type=F32)
        top = jnp.broadcast_to(before, (8, 2 * rows))
        for j in range(first // tile, last // tile):
            here = scores[j * tile : (j + 1) * tile, :]
            if j * tile >= old:
                here = here + jnp.concatenate([bias[kinds[0]], bias[kinds[1]]], axis=1)
                scores[j * tile : (j + 1) * tile, :] = here
            for i in range(0, tile, 8):
                top = jnp.maximum(top, here[i : i + 8])
        top = jnp.max(top, axis=0, keepdims=True)
        for j in range(first // tile, last // tile):
            here = scores[j * tile : (j + 1) * tile, :]
            probs[j * tile : (j + 1) * tile, :] = jnp.exp2((here - top) * rate).astype(BF16)
        both = jnp.dot(vt[:, first:last], probs[first:last, :], preferred_element_type=F32)
        fade = jnp.exp2((before - top) * rate)
        for owner, cols in ((one, slice(0, rows)), (two, slice(rows, 2 * rows))):
            st_num[owner] = st_num[owner] * fade[:, cols] + both[0:HD, cols]
            st_stat[owner, 1:2, :] = st_stat[owner, 1:2, :] * fade[:, cols] + both[HD : HD + 1, cols]
            st_stat[owner, 0:1, :] = top[:, cols]

    def open_blocks(one, two):
        for owner in (one, two):
            st_num[owner] = jnp.zeros((HD, rows), F32)
            st_stat[owner] = jnp.where(lax.broadcasted_iota(jnp.int32, (8, rows), 0) == 0, LOW, 0.0)
        attend(one, two, (0, 0), 0, deep)

    kk[0:deep, :] = ck_ref[...]
    values_in(0, cv_ref)
    vt[HD:, 0:old] = jnp.ones((16, old), BF16)
    line = lax.broadcasted_iota(jnp.int32, (NY * slots, rows), 0)
    which = line // slots
    key_y = y + jnp.where(which == 0, 0, jnp.where(which == 1, NY - 1, which - 1))
    key_y = jnp.where(key_y >= NY, key_y - NY, key_y)
    query_pos = jnp.broadcast_to(jnp.concatenate([pos_ref[...].astype(F32)] * group, axis=1), (rows, rows))
    same = (which == 0) & (line < count) & (query_pos.T <= query_pos)
    bias[0] = jnp.zeros((NY * slots, rows), F32)
    bias[1] = jnp.full((NY * slots, rows), -jnp.inf, F32)
    bias[2] = jnp.where((key_y < y) | same, 0.0, -jnp.inf)
    empty = jnp.where(lax.broadcasted_iota(jnp.int32, (HD + 16, part), 0) == HD, LOW, 0.0).astype(BF16)
    for piece in range(PIECES):
        for lane in (0, 1):
            pin[lane, 0, piece] = empty
            min_[lane, 0, piece] = empty
        min_[1, 1, piece] = empty

    line = lax.broadcasted_iota(jnp.int32, (16, part), 0)

    def state_of(owner, piece):
        here = slice(piece * part, (piece + 1) * part)
        return st_num[owner, :, here], st_stat[owner, 1:2, here], st_stat[owner, 0:1, here]

    def merge(state, message):
        num, den, top = state
        stat = message[HD:].astype(F32)
        top_in = stat[0:1] + stat[1:2] + stat[2:3]
        den_in = stat[3:4] + stat[4:5] + stat[5:6]
        best = jnp.maximum(top, top_in)
        mine = jnp.exp2((top - best) * rate)
        theirs = jnp.exp2((top_in - best) * rate)
        return num * mine + message[0:HD].astype(F32) * theirs, den * mine + den_in * theirs, best

    def three(value):
        one = value.astype(BF16).astype(F32)
        two = (value - one).astype(BF16).astype(F32)
        return one, two, value - one - two

    def message_of(state):
        num, den, top = state
        stat = jnp.zeros((16, part), F32)
        for k, value in enumerate(three(top) + three(den)):
            stat = jnp.where(line == k, value, stat)
        return num.astype(BF16), stat.astype(BF16)

    def hop_of(lane, step):
        return 1 if lane == 0 else jnp.where(step == near - 1, near + 1, 1)

    def p_copy(lane, step, piece):
        return remote(
            pout.at[lane, step, piece], pin.at[lane, step + 1, piece],
            psend.at[lane, step, piece], precv.at[lane, step + 1, piece], at_z(z + hop_of(lane, step)),
        )

    def m_copy(lane, step, piece):
        return remote(
            mout.at[lane, step, piece], min_.at[lane, step + 1, piece],
            msend.at[lane, step, piece], mrecv.at[lane, step + 1, piece], at_z(z - hop_of(lane, step)),
        )

    def turn(step, carry):
        back = step - near

        def kind_of(owner):
            return jnp.where(owner == z, 2, jnp.where(z < owner, 0, 1))

        def p_step(lane, piece):
            owner = wrap(z + near * (lane + 1) - back)
            num, stat = message_of(merge(state_of(owner, piece), pin[lane, back, piece]))
            pout[lane, back, piece, 0:HD, :] = num
            pout[lane, back, piece, HD:, :] = stat
            p_copy(lane, back, piece).start()

        def m_step(lane, piece):
            owner = wrap(z - near * (lane + 1) + back)
            num, stat = message_of(merge(state_of(owner, piece), min_[lane, back, piece]))
            mout[lane, back, piece, 0:HD, :] = num
            mout[lane, back, piece, HD:, :] = stat
            m_copy(lane, back, piece).start()

        @pl.when(step < near)
        def _():
            for lane in (0, 1):
                below_z = wrap(z - step - 1 - lane * near)
                above_z = wrap(z + step + 1 + lane * near)
                for piece in range(PIECES):
                    q_copy(0, lane, step, piece, below_z).wait_recv()

                    @pl.when(step + 1 < near)
                    def _():
                        q_copy(0, lane, step + 1, piece, below_z).start()

                    @pl.when(step + lane < near)
                    def _():
                        q_copy(1, lane, step, piece, above_z).wait_recv()

                    @pl.when(step + 1 + lane < near)
                    def _():
                        q_copy(1, lane, step + 1, piece, above_z).start()

        @pl.when(step >= near)
        def _():
            for lane in (1, 0):
                for piece in range(PIECES):

                    @pl.when(back >= 1)
                    def _():
                        p_copy(lane, back - 1, piece).wait_recv()

                    p_step(lane, piece)

                    @pl.when(back >= 1 + lane)
                    def _():
                        m_copy(lane, back - 1, piece).wait_recv()

                    @pl.when(back >= lane)
                    def _():
                        m_step(lane, piece)

        @pl.when(step == min(1, near - 2))
        def _():
            for i in (0, 1):
                y_copy(0, i).wait_recv()
                f_copy(i).start()

        @pl.when(step == min(2, near - 2))
        def _():
            for i in (2, 3):
                y_copy(1, i).wait_recv()
                f_copy(i).start()
            for i in (2, 3):
                y_copy(0, i).wait_recv()
            values_in(1, vbuf.at[1])
            for i in (0, 1):
                y_copy(1, i).wait_recv()
            values_in(2, vbuf.at[2])

        @pl.when(step == near - 1)
        def _():
            for i in range(4):
                f_copy(i).wait_recv()
            values_in(3, vbuf.at[3])
            turned = jnp.concatenate([nvbuf[k].astype(F32) for k in range(NY)], axis=0).T.astype(BF16)
            vt[:, old:keys] = turned[0 : HD + 16, :]

        @pl.when(step < near)
        def _():
            def open_pair(lane, carry):
                far = step + 1 + lane * near
                open_blocks(wrap(z - far), jnp.where(far == 2 * near, z, wrap(z + far)))
                return carry

            lax.fori_loop(0, 2, open_pair, 0)

        @pl.when((step >= near - 1) & (step < 2 * near - 1))
        def _():
            ahead = step - near + 1

            def rest(which, carry):
                one = jnp.where(ahead == 0, 2 * near, near - ahead)
                two = jnp.where(ahead == 0, near, ahead - near)
                three = jnp.where(ahead == 0, -near, ahead - 2 * near)
                four = jnp.where(ahead == near - 1, 0, 2 * near - 1 - ahead)
                one = wrap(z + jnp.where(which == 0, one, three))
                two = wrap(z + jnp.where(which == 0, two, four))
                attend(one, two, (kind_of(one), kind_of(two)), deep, keys)
                return carry

            lax.fori_loop(0, 2, rest, 0)

        return carry

    lax.fori_loop(0, 2 * near, turn, 0)

    home = []
    for piece in range(PIECES):
        state = state_of(z, piece)
        for lane in (0, 1):
            p_copy(lane, near - 1, piece).wait_recv()
            state = merge(state, pin[lane, near, piece])
            m_copy(lane, near - 1, piece).wait_recv()
            state = merge(state, min_[lane, near, piece])
        num, den, _ = state
        home.append(num / den)
    place = lax.broadcasted_iota(jnp.int32, (rows, HD), 0) % slots
    result = jnp.where(place < count, jnp.concatenate(home, axis=1).T, 0.0)

    take = slots // nh
    for j in range(nh):
        block = [result[g * slots + j * take : g * slots + (j + 1) * take] for g in range(group)]
        if take < 16:
            wide = [jnp.concatenate(block[: group // 2], axis=1), jnp.concatenate(block[group // 2 :], axis=1)]
            give[j] = jnp.concatenate(wide, axis=0).astype(BF16)
        else:
            give[j] = jnp.concatenate(block, axis=1).astype(BF16)

    def a_copy(k, to, slot_there):
        return remote(give.at[to], got.at[slot_there], asend.at[k], arecv.at[k], (ctx, to))

    for k in range(1, nh):
        a_copy(k, lax.rem(head + k, nh), head).start()
    got[head] = give[head]
    for k in range(1, nh):
        a_copy(k, lax.rem(head + k, nh), lax.rem(head + nh - k, nh)).wait_recv()
    out = []
    for j in range(nh):
        block = got[j].astype(F32)
        out += [block[0:take], block[take:]] if take < 16 else [block]
    out_ref[...] = jnp.concatenate(out, axis=1).astype(BF16)

    for k in range(1, nh):
        a_copy(k, lax.rem(head + k, nh), head).wait_send()
    for way in (0, 1):
        for i in range(4):
            y_copy(way, i).wait_send()
        for lane in (0, 1):
            for step in range(near - way * lane):
                for piece in range(PIECES):
                    q_copy(way, lane, step, piece, z).wait_send()
    for i in range(4):
        f_copy(i).wait_send()

    for lane in (0, 1):
        for step in range(near):
            for piece in range(PIECES):
                p_copy(lane, step, piece).wait_send()
                if step >= lane:
                    m_copy(lane, step, piece).wait_send()


def solution(mesh):
    n_ctx, nh = mesh.shape["ctx"], mesh.shape["head"]
    nz = n_ctx // NY
    near = nz // 4

    def local(queries, cache_k, cache_v, new_k, new_v, counts, positions):
        slots = queries.shape[0]
        group = queries.shape[1] // HD
        rows = slots * group
        deep = cache_k.shape[0]
        keys = NY * (deep + slots)
        take = slots // nh
        block = (2 * take, group * HD // 2) if take < 16 else (take, group * HD)
        message = (PIECES, HD + 16, rows // PIECES)
        vmem = pl.BlockSpec(memory_space=pltpu.VMEM)
        dma = pltpu.SemaphoreType.DMA
        return pl.pallas_call(
            functools.partial(kernel, nz, nh),
            out_shape=jax.ShapeDtypeStruct((take, nh * group * HD), BF16),
            in_specs=[vmem] * 5 + [pl.BlockSpec(memory_space=pltpu.SMEM), vmem],
            out_specs=vmem,
            scratch_shapes=[
                pltpu.VMEM((nz, HD, rows), BF16),
                pltpu.VMEM((keys, HD), BF16),
                pltpu.VMEM((NY, deep, HD), BF16),
                pltpu.VMEM((NY, slots, 2 * HD), BF16),
                pltpu.VMEM((HD + 16, keys), BF16),
                pltpu.VMEM((3, NY * slots, rows), F32),
                pltpu.VMEM((keys, 2 * rows), F32),
                pltpu.VMEM((keys, 2 * rows), BF16),
                pltpu.VMEM((nz, HD, rows), F32),
                pltpu.VMEM((nz, 8, rows), F32),
                pltpu.VMEM((2, near + 1) + message, BF16),
                pltpu.VMEM((2, near + 1) + message, BF16),
                pltpu.VMEM((2, near) + message, BF16),
                pltpu.VMEM((2, near) + message, BF16),
                pltpu.VMEM((nh,) + block, BF16),
                pltpu.VMEM((nh,) + block, BF16),
                dma((2, 2, near, PIECES)),
                dma((2, 2, near, PIECES)),
                dma((2, 4)),
                dma((2, 4)),
                dma((4,)),
                dma((4,)),
                dma((2, near, PIECES)),
                dma((2, near + 1, PIECES)),
                dma((2, near, PIECES)),
                dma((2, near + 1, PIECES)),
                dma((nh,)),
                dma((nh,)),
            ],
            compiler_params=pltpu.CompilerParams(
                collective_id=0, has_side_effects=True, vmem_limit_bytes=56 * 1024 * 1024
            ),
        )(
            queries, cache_k, cache_v, new_k, new_v, counts,
            positions.reshape(1, slots),
        )

    spec = P("ctx", "head")
    return jax.shard_map(
        local,
        mesh=mesh,
        in_specs=(spec, spec, spec, spec, spec, P("ctx"), P("ctx")),
        out_specs=P(("ctx", "head"), None),
        check_vma=False,
    )
```

time: 1540 us -> 75.1 us (0.05); the launches traced: 1520 us -> 74.9 us
  starting transfers between devices: 825 us -> 0 us
  waiting for transfers between devices: 366 us -> 0 us
  blocking collectives: 152 us -> 0 us
  Pallas kernels: 0 us -> 72.7 us
  other arithmetic: 66.2 us -> 0 us
  matrix products: 64.4 us -> 0 us
  local copies, waits for them, and re-layouts: 38.9 us -> 1.47 us
    ppermute x320 -> x0, starting transfers between devices: 825 us -> none  [from_behind(): return lax.ppermute(value, axis, pairs)]
    ppermute x320 -> x0, waiting for transfers between devices: 366 us -> none  [from_behind(): return lax.ppermute(value, axis, pairs)]
    all_to_all x1 -> x0, blocking collectives: 152 us -> none  [local(): lax.all_to_all(result, 'head', split_axis=0, concat_axis=1, tiled=True)]
    pallas_call x0 -> x1, Pallas kernels: none -> 72.7 us  [local(): pl.pallas_call(functools.partial(kernel, nz, nh), out_shape=jax.ShapeDtyp...]
    dot_general x256 -> x0, matrix products: 64.4 us -> none  [the longest x128 31.6 us: absorb(): jnp.einsum('rjgk,kjd->rjgd', weights.astype(jnp.bfloat16), vals, preferre...]
    lt x65 -> x0, other arithmetic: 41.7 us -> none  [local(): key_live = jnp.arange(slots, dtype=jnp.int32) < counts[0]]
    while x321 -> x0, local copies, waits for them, and re-layouts: 28 us -> none
    reduce_sum x128 -> x0, other arithmetic: 16.8 us -> none  [absorb(): denom = denom * factor + jnp.sum(weights, axis=-1)]
  transfers between devices with their start and end apart: 320 -> 0, of which waited for: 73 -> 0; matrix products, arithmetic and copies ran while one was open for 0% -> 0% of each run, Pallas kernels for 0% -> 0%
where the time goes in v1:
time: 75.1 us; the launch traced here: 74.9 us
  Pallas kernels  72.7 us (97%)
  local copies, waits for them, and re-layouts  1.47 us (2%)
    pallas_call x1, Pallas kernels, local(): pl.pallas_call(functools.partial(kernel, nz, nh), out_shape=jax.ShapeDtyp...  72.7 us

profile of v1, /device:TPU:1, one launch (start us, length us, event | category | flops | bytes accessed | tf_op | source)
XLA Modules:
  0.0 74.9 jit_solution(88102918447114506)
XLA Ops:
  0.7 72.7 %shard_map.73 = bf16[8,4096]{1,0:T(8,128)(2,1)} custom-call(bf16[64,512]{1,0:T(8,128)(2,1)} %q_ref.1, bf16[512,128]{1,0:T(8,128)(2,1)} %ck_ref.1, bf16[512,128]{1,0:T(8,128)(2,1)} %cv_ref.1, bf16[64,128]{1,0:T(8,128)(2,1)} %nk_ref.1, bf16[64,128]{1,0:T(8,128)(2,1)} %nv_ref.1, s32[1]{0:T(128)S(6)} %copy.9.count_ref, s32[1,64]{1,0:T(1,128)} %bitcast.1), custom_call_target="tpu_custom_call" | custom-call | tf_op jit(solution)/shard_map/pallas_call | solution.py:385
  73.4 1.5 %copy.10 = bf16[8,4096]{1,0:T(8,128)(2,1)} copy(bf16[8,4096]{1,0:T(8,128)(2,1)} %shard_map.73) | data formatting | bytes 131072

commit v2 on v1

--- a/solution.py
+++ b/solution.py
@@ -15,6 +15,7 @@
 BF16 = jnp.bfloat16
 LOW = -1e30
 PIECES = 2
+CHUNK = 64
 
 
 def kernel(
@@ -32,7 +33,6 @@
     keys = old + NY * slots
     part = rows // PIECES
     depth = HD // PIECES
-    tile = 2 * HD
     ctx = lax.axis_index("ctx")
     head = lax.axis_index("head")
     z = ctx // NY
@@ -110,17 +110,17 @@
         before = jnp.concatenate([st_stat[one, 0:1, :], st_stat[two, 0:1, :]], axis=1)
         scores[first:last, :] = jnp.dot(kk[first:last, :], wide, preferred_element_type=F32)
         top = jnp.broadcast_to(before, (8, 2 * rows))
-        for j in range(first // tile, last // tile):
-            here = scores[j * tile : (j + 1) * tile, :]
-            if j * tile >= old:
-                here = here + jnp.concatenate([bias[kinds[0]], bias[kinds[1]]], axis=1)
-                scores[j * tile : (j + 1) * tile, :] = here
-            for i in range(0, tile, 8):
+        for j in range(first, last, CHUNK):
+            here = scores[j : j + CHUNK, :]
+            if j >= old:
+                hidden = [bias[kind, j - old : j - old + CHUNK, :] for kind in kinds]
+                here = here + jnp.concatenate(hidden, axis=1)
+                scores[j : j + CHUNK, :] = here
+            for i in range(0, CHUNK, 8):
                 top = jnp.maximum(top, here[i : i + 8])
         top = jnp.max(top, axis=0, keepdims=True)
-        for j in range(first // tile, last // tile):
-            here = scores[j * tile : (j + 1) * tile, :]
-            probs[j * tile : (j + 1) * tile, :] = jnp.exp2((here - top) * rate).astype(BF16)
+        for j in range(first, last, CHUNK):
+            probs[j : j + CHUNK, :] = jnp.exp2((scores[j : j + CHUNK, :] - top) * rate).astype(BF16)
         both = jnp.dot(vt[:, first:last], probs[first:last, :], preferred_element_type=F32)
         fade = jnp.exp2((before - top) * rate)
         for owner, cols in ((one, slice(0, rows)), (two, slice(rows, 2 * rows))):

time: 75.1 us -> 75 us (level)
  no operation moved by 1% of the time
where the time goes in v2:
time: 75 us; the launch traced here: 74.8 us
  Pallas kernels  72.7 us (97%)
  local copies, waits for them, and re-layouts  1.47 us (2%)
    pallas_call x1, Pallas kernels, local(): pl.pallas_call(functools.partial(kernel, nz, nh), out_shape=jax.ShapeDtyp...  72.7 us

profile of v2, /device:TPU:1, one launch (start us, length us, event | category | flops | bytes accessed | tf_op | source)
XLA Modules:
  0.0 74.8 jit_solution(14479458186752657843)
XLA Ops:
  0.7 72.7 %shard_map.73 = bf16[8,4096]{1,0:T(8,128)(2,1)} custom-call(bf16[64,512]{1,0:T(8,128)(2,1)} %q_ref.1, bf16[512,128]{1,0:T(8,128)(2,1)} %ck_ref.1, bf16[512,128]{1,0:T(8,128)(2,1)} %cv_ref.1, bf16[64,128]{1,0:T(8,128)(2,1)} %nk_ref.1, bf16[64,128]{1,0:T(8,128)(2,1)} %nv_ref.1, s32[1]{0:T(128)S(6)} %copy.9.count_ref, s32[1,64]{1,0:T(1,128)} %bitcast.1), custom_call_target="tpu_custom_call" | custom-call | tf_op jit(solution)/shard_map/pallas_call | solution.py:385
  73.4 1.5 %copy.10 = bf16[8,4096]{1,0:T(8,128)(2,1)} copy(bf16[8,4096]{1,0:T(8,128)(2,1)} %shard_map.73) | data formatting | bytes 131072
